TPU v7x, 512 devices: a whole 4x8x8 slice. The times are simulated.
512 devices in a mesh: dp: 16 (over z, y_lo), tile: 32 (over x, y_hi, core).
Axes of the slice: x: 4, y: 8 (y_hi: 4, y_lo: 2; y = y_hi * 2 + y_lo), z: 8, core: 2. Of those that a mesh axis runs over, the one named last changes fastest.
Arguments:
- acts: bfloat16 [2048, 4096], P('dp', 'tile'), may hold values from -64 to 64
- grads: bfloat16 [2048, 14336], P('dp', 'tile'), may hold values from -64 to 64
- basis_in: bfloat16 [4096, 4096], P('tile', 'dp'), may hold values from -0.09375 to 0.09375
- basis_out: bfloat16 [14336, 14336], P('dp', 'tile'), may hold values from -0.046875 to 0.046875
Outputs:
- act_cov: float32 [4096, 4096], P('tile', 'dp')
- grad_cov: float32 [14336, 14336], P('tile', 'dp')
- corrections: float32 [14336, 4096], P('tile', 'dp')
All inputs are finite; a program needn't handle non-finite values.
Results may differ from a plain program's by a relative error of at most 0.0006.
Values may be sent and summed in bfloat16 or wider, within the bound.
A program may use at most 64 MiB of HBM per device.

v0:
```python
import jax
import jax.numpy as jnp
from jax import lax
from jax.sharding import PartitionSpec as P


def from_root(array, axis, root):
    mine = lax.axis_index(axis) == root
    return lax.psum(jnp.where(mine, array, jnp.zeros_like(array)), axis)


def outer_sum(left, right):
    return lax.dot_general(
        left, right, (((0,), (0,)), ((), ())), preferred_element_type=jnp.float32
    )


def body(acts, grads, basis_in, basis_out):
    ratio = lax.axis_size("tile") // lax.axis_size("dp")
    first = lax.axis_index("dp") * ratio
    act_rows, grad_rows = (
        lax.all_gather(acts, "dp", axis=0, tiled=True),
        lax.all_gather(grads, "dp", axis=0, tiled=True),
    )
    tokens = act_rows.shape[0]
    scale = 1.0 / tokens
    act_parts = []
    grad_parts = []
    for offset in range(ratio):
        act_piece, grad_piece = (
            from_root(act_rows, "tile", first + offset),
            from_root(grad_rows, "tile", first + offset),
        )
        act_parts.append(act_piece)
        grad_parts.append(grad_piece)
    act_cols = jnp.concatenate(act_parts, axis=1)
    grad_cols = jnp.concatenate(grad_parts, axis=1)
    act_cov = outer_sum(act_rows, act_cols) * scale
    grad_cov = outer_sum(grad_rows, grad_cols) * scale
    share_out = lax.psum_scatter(
        jnp.dot(grad_cols, basis_out, preferred_element_type=jnp.float32),
        "dp",
        scatter_dimension=0,
        tiled=True,
    )
    square_out = (share_out * share_out).astype(jnp.bfloat16)
    sq_out = lax.all_gather(square_out, "dp", axis=0, tiled=True)
    token_share = lax.all_to_all(act_rows, "tile", split_axis=0, concat_axis=1, tiled=True)
    share_in = jnp.dot(
        token_share,
        lax.all_gather(basis_in, "tile", axis=0, tiled=True),
        preferred_element_type=jnp.float32,
    )
    square_in = (share_in * share_in).astype(jnp.bfloat16)
    sq_in = lax.all_gather(square_in, "tile", axis=0, tiled=True)
    corrections = outer_sum(sq_out, sq_in) * scale
    return (act_cov, grad_cov, corrections)


def solution(mesh):
    in_specs = (P("dp", "tile"), P("dp", "tile"), P("tile", "dp"), P("dp", "tile"))
    out_specs = (P("tile", "dp"), P("tile", "dp"), P("tile", "dp"))
    return jax.shard_map(body, mesh=mesh, in_specs=in_specs, out_specs=out_specs, check_vma=False)
```

profile of v0, /device:TPU:1, one launch (start us, length us, event | category | flops | bytes accessed | tf_op | source)
XLA Modules:
  0.0 705.2 jit_solution(16357979697610752225)
XLA Ops:
  7.2 0.0 copy-start
  7.2 0.0 all-gather.5.cloned.1.call-start
  7.2 0.7 all-gather.5.cloned.1.call-update
  7.9 0.0 all-reduce.3.cloned.1.call-start
  8.0 40.8 %all_gather.15 = bf16[2048,128]{1,0:T(8,128)(2,1)S(1)} all-gather(bf16[128,128]{1,0:T(8,128)(2,1)} %param.4), channel_id=1, replica_groups=mesh['dp'=16,'tile'=32] {'dp'}, dimensions={0}, use_global_device_ids=true | all-gather | bytes 557056 | tf_op jit(solution)/shard_map/all_gather | solution.py:22
  48.8 1.1 broadcast_select_fusion.3
  49.9 37.0 %all-gather.5.cloned.1.call-done = bf16[2048,448]{0,1:T(8,128)(2,1)} async-done(((bf16[128,448]{0,1:T(8,128)(2,1)}), bf16[2048,448]{0,1:T(8,128)(2,1)}) %all-gather.5.cloned.1.call-update) | async-done | bytes 1835024 | tf_op jit(solution)/shard_map/all_gather | solution.py:23
  86.9 3.6 broadcast_select_fusion
  90.5 0.0 all-reduce.3.cloned.1.call-update
  90.5 0.0 all-gather.9.cloned.1.call-start
  90.6 0.7 all-gather.9.cloned.1.call-update
  91.2 0.0 reduce-scatter.2.cloned.1.call-start
  91.3 314.3 %all-reduce.3.cloned.1.call-done = (bf16[2048,128]{1,0:T(8,128)(2,1)}, bf16[2048,128]{1,0:T(8,128)(2,1)}, bf16[2048,448]{0,1:T(8,128)(2,1)}, bf16[2048,448]{0,1:T(8,128)(2,1)}) async-done(((bf16[2048,128]{1,0:T(8,128)(2,1)}, bf16[2048,128]{1,0:T(8,128)(2,1)}, bf16[2048,448]{0,1:T(8,128)(2,1)}, bf16[2048,448]{0,1:T(8,128)(2,1)}), (bf16[2048,128]{1,0:T(8,128)(2,1)}, bf16[2048,128]{1,0:T(8,128)(2,1)}, ...) | async-done | bytes 4718608 | tf_op jit(solution)/shard_map/psum | solution.py:9
  405.6 0.0 copy-start.1
  405.6 1.8 constant_dynamic-update-slice_fusion.1
  407.4 0.3 copy-done.1
  407.7 0.2 constant_dynamic-update-slice_fusion
  407.9 0.0 copy-start.3
  407.9 1.8 copy-done.3
  409.7 0.0 copy-done
  409.7 3.9 fusion.8
  413.6 0.0 reduce-scatter.2.cloned.1.call-update
  413.6 0.0 all-gather.11.cloned.1.call-start
  413.7 25.9 %all_to_all.19 = bf16[32,64,128]{2,1,0:T(8,128)(2,1)S(1)} all-to-all(bf16[32,64,128]{2,1,0:T(8,128)(2,1)S(1)} %bitcast.21), channel_id=1, replica_groups=mesh['dp'=16,'tile'=32] {'tile'}, dimensions={0} | all-to-all | bytes 1048576 | tf_op jit(solution)/shard_map/all_to_all | solution.py:48
  439.6 35.3 %all-gather.9.cloned.1.call-done = bf16[4096,256]{1,0:T(8,128)(2,1)} async-done(((bf16[128,256]{1,0:T(8,128)(2,1)}), bf16[4096,256]{1,0:T(8,128)(2,1)}) %all-gather.9.cloned.1.call-update) | async-done | bytes 2097168 | tf_op jit(solution)/shard_map/all_gather | solution.py:51
  474.9 2.7 fusion.1
  477.6 0.0 copy-start.2
  477.6 0.0 all-gather.11.cloned.1.call-update
  477.6 0.0 all-gather.7.cloned.1.call-start
  477.6 90.4 %reduce-scatter.2.cloned.1.call-done = f32[128,448]{0,1:T(8,128)} async-done(((f32[2048,448]{0,1:T(8,128)}), f32[128,448]{0,1:T(8,128)}) %reduce-scatter.2.cloned.1.call-update) | async-done | bytes 229392 | tf_op jit(solution)/shard_map/reduce_scatter | solution.py:40
  568.0 1.6 multiply_convert_fusion
  569.6 0.0 all-gather.7.cloned.1.call-update
  569.6 1.7 fusion
  571.3 0.8 copy.11
  572.1 0.0 copy-done.2
  572.1 5.3 multiply_bitcast_fusion
  577.3 49.9 %all-gather.11.cloned.1.call-done = bf16[2048,256]{1,0:T(8,128)(2,1)} async-done(((bf16[64,256]{1,0:T(8,128)(2,1)}), bf16[2048,256]{1,0:T(8,128)(2,1)}) %all-gather.11.cloned.1.call-update) | async-done | bytes 1048592 | tf_op jit(solution)/shard_map/all_gather | solution.py:55
  627.3 67.9 %all-gather.7.cloned.1.call-done = bf16[2048,448]{0,1:T(8,128)(2,1)} async-done(((bf16[128,448]{0,1:T(8,128)(2,1)}), bf16[2048,448]{0,1:T(8,128)(2,1)}) %all-gather.7.cloned.1.call-update) | async-done | bytes 1835024 | tf_op jit(solution)/shard_map/all_gather | solution.py:47
  695.2 3.2 convolution_multiply_fusion
Async XLA Ops:
  7.2 402.5 %copy-start = (bf16[896,448]{0,1:T(8,128)(2,1)S(1)}, bf16[896,448]{0,1:T(8,128)(2,1)}, u32[]{:S(2)}) copy-start(bf16[896,448]{0,1:T(8,128)(2,1)} %param.7) | copy-start | bytes 2408452
  7.2 79.7 %all-gather.5.cloned.1.call-start = ((), (), s32[]{:S(2)}) async-start(), calls=%async_computation.2 | async-start | bytes 1949696 | tf_op jit(solution)/shard_map/all_gather | solution.py:23
  7.9 397.7 %all-reduce.3.cloned.1.call-start = ((), (), s32[]{:S(2)}) async-start(), calls=%async_computation.7 | async-start | bytes 9437184 | tf_op jit(solution)/shard_map/psum | solution.py:9
  90.5 384.4 %all-gather.9.cloned.1.call-start = ((), (), s32[]{:S(2)}) async-start(), calls=%async_computation.5 | async-start | bytes 2162688 | tf_op jit(solution)/shard_map/all_gather | solution.py:51
  91.2 476.8 %reduce-scatter.2.cloned.1.call-start = ((), (), s32[]{:S(2)}) async-start(), calls=%async_computation.3 | async-start | bytes 3899392 | tf_op jit(solution)/shard_map/reduce_scatter | solution.py:40
  405.6 2.1 copy-start.1
  407.9 1.8 copy-start.3
  413.6 213.6 %all-gather.11.cloned.1.call-start = ((), (), s32[]{:S(2)}) async-start(), calls=%async_computation.6 | async-start | bytes 1081344 | tf_op jit(solution)/shard_map/all_gather | solution.py:55
  477.6 94.5 %copy-start.2 = (bf16[2048,448]{0,1:T(8,128)(2,1)S(1)}, bf16[2048,448]{0,1:T(8,128)(2,1)}, u32[]{:S(2)}) copy-start(bf16[2048,448]{0,1:T(8,128)(2,1)} %all-gather.5.cloned.1.call-done) | copy-start | bytes 5505028
  477.6 217.6 %all-gather.7.cloned.1.call-start = ((), (), s32[]{:S(2)}) async-start(), calls=%async_computation.4 | async-start | bytes 1949696 | tf_op jit(solution)/shard_map/all_gather | solution.py:47
Sparse Core Ops, SparseCore 0:
  10.0 76.8 all-gather.4
  90.7 314.9 all-reduce.2
  408.8 66.0 all-gather.8
  477.6 90.3 reduce-scatter.1
  571.0 56.2 all-gather.10
  629.7 65.4 all-gather.6
where the time goes:
time: 715 us; the launch traced here: 705 us
  waiting for transfers between devices  596 us (83%)
  blocking collectives  66.7 us (9%)
  matrix products  16.8 us (2%)
  between operations  14.2 us (2%)
    psum x1, waiting for transfers between devices, from_root(): return lax.psum(jnp.where(mine, array, jnp.zeros_like(array)), axis)  314 us
    reduce_scatter x1, waiting for transfers between devices, body(): lax.psum_scatter(jnp.dot(grad_cols, basis_out, preferred_element_type=jnp...  90.4 us
    all_gather x1, waiting for transfers between devices, body(): sq_out = lax.all_gather(square_out, 'dp', axis=0, tiled=True)  67.9 us
    all_gather x1, waiting for transfers between devices, body(): sq_in = lax.all_gather(square_in, 'tile', axis=0, tiled=True)  49.9 us
    all_gather x1, blocking collectives, body(): lax.all_gather(acts, 'dp', axis=0, tiled=True)  40.8 us
    all_gather x1, waiting for transfers between devices, body(): lax.all_gather(grads, 'dp', axis=0, tiled=True)  37 us
    all_gather x1, waiting for transfers between devices, body(): lax.all_gather(basis_in, 'tile', axis=0, tiled=True)  35.3 us
    all_to_all x1, blocking collectives, body(): lax.all_to_all(act_rows, 'tile', split_axis=0, concat_axis=1, tiled=True)  25.9 us
  transfers between devices with their start and end apart: 6, of which 6 were waited for; matrix products, arithmetic and copies ran while one was open for 3% of the time, Pallas kernels for 0%

commit v1 on v0

v1 whole, which is shorter than its diff:
```python
import functools

import jax
import jax.numpy as jnp
from jax import lax
from jax.experimental import pallas as pl
from jax.experimental.pallas import tpu as pltpu
from jax.sharding import PartitionSpec as P

MESH = pl.DeviceIdType.MESH
F32 = jnp.float32
BF16 = jnp.bfloat16

G = 448
A = 128
R = G + A
Q = R // 4
B = 128
NB = 16
GH = G // 2
RH = R // 2

CHAIN = 1
K1, K2, K3 = 1, 2, 3
T_AT = (2, 5, 8, 11)
STEPS = 8 + 3 * CHAIN + K3


def mod(a, n):
    return (a + n) % n


def nt(a, b):
    return lax.dot_general(a, b, (((1,), (1,)), ((), ())), preferred_element_type=F32)


def nn(a, b):
    return lax.dot_general(a, b, (((1,), (0,)), ((), ())), preferred_element_type=F32)


def arrived(ref, sem):
    pltpu.make_async_copy(ref, ref, sem).wait()


def offset(g):
    half = (g + 1) // 2
    return 4 + half * (1 - 2 * (g % 2))


def kernel(
    acts, grads, basis_in, basis_out, act_cov, grad_cov, corr,
    xk, a1, xd, bt, bit, pf, pb, rb, rsu, rsd, sq, pio, pis, pir, px, py, si,
    a1_s, a1_r, own_sem, d2_s, y_r, ch_s, x_s, x_r, x2_s, x2_r, c_s, c_r,
    tp_s, tp_r, t_s, t_r, pr_s, pr_r, rs_s, rs_r, gp_s, gp_r, g_s, g_r,
    in_s, in_r,
):
    dp, tile = lax.axis_index("dp"), lax.axis_index("tile")
    z, yl = dp // 2, dp % 2
    k, c = tile // 2, tile % 2
    x, yh = k // 4, k % 4
    up, down = mod(z + 1, 8), mod(z + 7, 8)

    def at(z=z, yl=yl, x=x, yh=yh, c=c):
        return (2 * z + yl, (4 * x + yh) * 2 + c)

    def remote(src, dst, ss, rs, dev):
        return pltpu.make_async_remote_copy(
            src_ref=src, dst_ref=dst, send_sem=ss, recv_sem=rs, device_id=dev, device_id_type=MESH
        )

    sent = []

    def send(src, dst, ss, rs, dev):
        remote(src, dst, ss, rs, dev).start()
        sent.append((src, ss))

    xk[dp, 0:G] = grads[...].T
    xk[dp, G:R] = acts[...].T

    barrier = pltpu.get_barrier_semaphore()

    def greet(j, carry):
        pl.semaphore_signal(barrier, inc=1, device_id=(mod(dp + j, 16), tile), device_id_type=MESH)
        return carry

    lax.fori_loop(1, 16, greet, 0)
    for j in range(1, 4):
        pl.semaphore_signal(barrier, inc=1, device_id=at(x=mod(x + j, 4)), device_id_type=MESH)
        pl.semaphore_signal(barrier, inc=1, device_id=at(yh=mod(yh + j, 4)), device_id_type=MESH)
    pl.semaphore_signal(barrier, inc=1, device_id=at(c=1 - c), device_id_type=MESH)
    pl.semaphore_wait(barrier, 22)

    def quarter(ref, q):
        return ref.at[pl.ds(pl.multiple_of(q * Q, 16), Q)]

    for j in range(1, 4):
        q = mod(x + j, 4)
        send(quarter(xk.at[dp], q), a1.at[x], a1_s.at[j - 1], a1_r.at[x], at(x=q))
    keep = pltpu.make_async_copy(quarter(xk.at[dp], x), a1.at[x], own_sem)
    keep.start()
    keep.wait()

    def plane_of(col):
        return 2 * col + yh // 2, yh % 2

    def to_plane(j, act):
        col = mod(x + j, 4)
        zt, yt = plane_of(col)
        here = jnp.logical_and(zt == z, yt == yl)
        src, dst = a1.at[col], quarter(xd.at[c, dp], x)

        @pl.when(here)
        def _():
            if act:
                pltpu.make_async_copy(src, dst, y_r.at[dp]).start()

        @pl.when(jnp.logical_not(here))
        def _():
            copy = remote(src, dst, d2_s.at[j], y_r.at[dp], at(z=zt, yl=yt))
            if act:
                copy.start()
            else:
                copy.wait_send()

    for j in range(4):
        if j:
            col = mod(x + j, 4)
            arrived(a1.at[col], a1_r.at[col])
        to_plane(j, True)

    def ring_send(buf, rows, s, r, h, y, act=True):
        eu = 2 * mod(z - h, 8) + y
        ed = 2 * mod(z + h, 8) + y
        lo = pl.ds(0, rows if h < 3 else rows // 2)
        hi = pl.ds(0, rows) if h < 3 else pl.ds(rows // 2, rows // 2)
        for n, ref, dev in ((0, buf.at[eu, lo], at(z=up)), (1, buf.at[ed, hi], at(z=down))):
            copy = remote(ref, ref, s.at[n, h, y], r.at[n, h, y], dev)
            copy.start() if act else copy.wait_send()

    def ring_wait(buf, rows, r, h, y):
        eu = 2 * mod(z - 1 - h, 8) + y
        ed = 2 * mod(z + 1 + h, 8) + y
        lo = pl.ds(0, rows if h < 3 else rows // 2)
        hi = pl.ds(0, rows) if h < 3 else pl.ds(rows // 2, rows // 2)
        arrived(buf.at[eu, lo], r.at[0, h, y])
        arrived(buf.at[ed, hi], r.at[1, h, y])

    def ring_hop(buf, rows, s, r, h):
        for y in (yl, 1 - yl):
            ring_wait(buf, rows, r, h - 1, y)
            if h < 4:
                ring_send(buf, rows, s, r, h, y)

    send(xk.at[dp], xk.at[dp], tp_s, tp_r, at(yl=1 - yl))
    ring_send(xk, R, t_s, t_r, 0, yl)

    bt[...] = basis_out[...].T
    bit[...] = basis_in[...].T
    partner = 2 * z + 1 - yl
    arrived(xk.at[partner], tp_r)
    ring_send(xk, R, t_s, t_r, 0, 1 - yl)

    root = 2 * (z % 2) + yl
    role = mod(yh - root, 4)
    hops = (role, mod(4 - role, 4))
    last = jnp.maximum(hops[0], hops[1])

    def stage(f, i, late):
        g = i - hops[f] * CHAIN - late
        e = 2 * mod(z + offset(g) + 8, 8) + f
        return jnp.logical_and(g >= 0, g < 8), e

    right, left = mod(x + 1, 4), mod(x + 3, 4)
    west, east = at(x=left), at(x=right)

    def spread(f, e, act):
        mine = quarter(xd.at[c, e], x)
        if act:
            arrived(mine, y_r.at[e])

        @pl.when(hops[f] < 3)
        def _():
            step = 1 if f == 0 else 3
            copy = remote(mine, mine, ch_s.at[e], y_r.at[e], at(yh=mod(yh + step, 4)))
            copy.start() if act else copy.wait_send()

        for n, dev in enumerate((east, west)):
            copy = remote(mine, mine, x_s.at[n, e], x_r.at[n, e], dev)
            copy.start() if act else copy.wait_send()

    def across(f, e, act):
        from_left, from_right = quarter(xd.at[c, e], left), quarter(xd.at[c, e], right)
        if act:
            arrived(from_left, x_r.at[0, e])
            arrived(from_right, x_r.at[1, e])
        ref, dev = (from_left, east) if f == 0 else (from_right, west)
        copy = remote(ref, ref, x2_s.at[e], x2_r.at[e], dev)
        copy.start() if act else copy.wait_send()

    def share(f, e, act):
        if act:
            arrived(quarter(xd.at[c, e], mod(x + 2, 4)), x2_r.at[e])
        copy = remote(xd.at[c, e], xd.at[c, e], c_s.at[e], c_r.at[e], at(c=1 - c))
        copy.start() if act else copy.wait_send()

    def project(g):
        zz = mod(z + offset(g) + 8, 8)
        cols = []
        for f in range(2):
            arrived(xd.at[1 - c, 2 * zz + f], c_r.at[2 * zz + f])
        for f in range(2):
            cols.append(jnp.concatenate([xd[0, 2 * zz + f, 0:G], xd[1, 2 * zz + f, 0:G]], axis=0))
        out = nn(bt[...], jnp.concatenate(cols, axis=1))
        first, second = out[:, 0:B], out[:, B : 2 * B]
        even = yl == 0
        pf[zz] = jnp.where(even, first, second)
        pb[zz] = jnp.where(even, second, first).astype(BF16)
        remote(pb.at[zz], rb.at[zz], pr_s.at[zz], pr_r.at[zz], at(yl=1 - yl)).start()

    def step(i, carry):
        for f in range(2):
            for late, work in ((0, spread), (K1, across), (K2, share)):
                valid, e = stage(f, i, late)

                @pl.when(valid)
                def _():
                    work(f, e, True)

        for n, when in enumerate(T_AT):

            @pl.when(i == when)
            def _():
                ring_hop(xk, R, t_s, t_r, n + 1)

        g = i - last * CHAIN - K3

        @pl.when(jnp.logical_and(g >= 0, g < 8))
        def _():
            project(g)

        return carry

    lax.fori_loop(0, STEPS, step, 0)

    def total(zz):
        arrived(rb.at[zz], pr_r.at[zz])
        return pf[zz] + rb[zz].astype(F32)

    far = mod(z + 4, 8)
    pf[far] = total(far)
    send(pf.at[far, 0:GH], rsu.at[0, 0:GH], rs_s.at[0, 0], rs_r.at[0, 0], at(z=up))
    send(pf.at[far, GH:G], rsd.at[0, GH:G], rs_s.at[1, 0], rs_r.at[1, 0], at(z=down))

    def reduce_step(s):
        for n, (buf, zz, dev) in enumerate(
            ((rsu, mod(z + 4 - s, 8), at(z=up)), (rsd, mod(z + 4 + s, 8), at(z=down)))
        ):
            pf[zz] = total(zz)
            rows = slice(0, G) if s > 1 else (slice(0, GH), slice(GH, G))[n]
            arrived(buf.at[s - 1, rows], rs_r.at[n, s - 1])
            pf[zz, rows] = pf[zz, rows] + buf[s - 1, rows]
            send(pf.at[zz], buf.at[s], rs_s.at[n, s], rs_r.at[n, s], dev)

    def project_in():
        mine = bit[pl.ds(pl.multiple_of(c * A, A), A)]
        other = bit[pl.ds(pl.multiple_of((1 - c) * A, A), A)]
        for e in range(0, NB, 4):
            cols = jnp.concatenate([xk[e + n, G:R] for n in range(4)], axis=1)
            for weights, ref in ((mine, pio), (other, pis)):
                out = nn(weights, cols)
                for n in range(4):
                    ref[e + n] = out[:, n * B : (n + 1) * B]
        send(pis, pir, in_s.at[0], in_r.at[0], at(c=1 - c))

    def in_over_x():
        arrived(pir, in_r.at[0])
        pio[...] = pio[...] + pir[...]
        for j in range(1, 4):
            q = mod(x + j, 4)
            send(pio.at[pl.ds(4 * q, 4)], px.at[x], in_s.at[j], in_r.at[1 + x], at(x=q))

    def in_over_y():
        mine = pl.ds(4 * x, 4)
        acc = pio[mine]
        for j in range(1, 4):
            q = mod(x + j, 4)
            arrived(px.at[q], in_r.at[1 + q])
            acc = acc + px[q]
        pio[mine] = acc
        for j in range(1, 4):
            w = mod(yh + j, 4)
            send(pio.at[4 * x + w], py.at[yh], in_s.at[3 + j], in_r.at[5 + yh], at(yh=w))

    def in_square():
        acc = pio[k]
        for j in range(1, 4):
            w = mod(yh + j, 4)
            arrived(py.at[w], in_r.at[5 + w])
            acc = acc + py[w]
        si[c, k] = (acc * acc).astype(BF16)
        for j in range(1, 4):
            w = mod(yh + j, 4)
            send(si.at[c, k], si.at[c, k], in_s.at[6 + j], in_r.at[9 + yh], at(yh=w))

    def in_gather_x():
        for j in range(1, 4):
            w = mod(yh + j, 4)
            arrived(si.at[c, 4 * x + w], in_r.at[9 + w])
        mine = si.at[c, pl.ds(4 * x, 4)]
        for j in range(1, 4):
            q = mod(x + j, 4)
            send(mine, mine, in_s.at[9 + j], in_r.at[13 + x], at(x=q))

    def in_share():
        for j in range(1, 4):
            q = mod(x + j, 4)
            arrived(si.at[c, pl.ds(4 * q, 4)], in_r.at[13 + q])
        send(si.at[c], si.at[c], in_s.at[13], in_r.at[17], at(c=1 - c))

    scale = 1.0 / (NB * B)

    def covariances(first):
        for e in (first, first + 4):
            blocks = range(e, e + 4)
            rows = jnp.concatenate([xk[n, 0:G] for n in blocks], axis=1)
            cols = jnp.concatenate(
                [jnp.concatenate([xd[0, n, 0:G], xd[1, n, 0:G]], axis=0) for n in blocks], axis=1
            )
            part = nt(rows, cols) * scale
            grad_cov[...] = part if e == 0 else grad_cov[...] + part
            rows = jnp.concatenate([xk[n, G:R] for n in blocks], axis=1)
            cols = jnp.concatenate(
                [jnp.concatenate([xd[0, n, G:R], xd[1, n, G:R]], axis=0) for n in blocks], axis=1
            )
            part = nt(rows, cols) * scale
            act_cov[...] = part if e == 0 else act_cov[...] + part

    project_in()
    reduce_step(1)
    in_over_x()
    reduce_step(2)
    covariances(0)
    reduce_step(3)
    in_over_y()

    arrived(rsu.at[3], rs_r.at[0, 3])
    arrived(rsd.at[3], rs_r.at[1, 3])
    mine = total(z) + rsu[3] + rsd[3]
    sq[dp] = (mine * mine).astype(BF16)

    send(sq.at[dp], sq.at[dp], gp_s, gp_r, at(yl=1 - yl))
    ring_send(sq, G, g_s, g_r, 0, yl)
    arrived(sq.at[partner], gp_r)
    ring_send(sq, G, g_s, g_r, 0, 1 - yl)
    in_square()
    ring_hop(sq, G, g_s, g_r, 1)
    in_gather_x()
    covariances(8)
    ring_hop(sq, G, g_s, g_r, 2)
    in_share()
    ring_hop(sq, G, g_s, g_r, 3)
    arrived(si.at[1 - c], in_r.at[17])
    ring_hop(sq, G, g_s, g_r, 4)

    for e in range(0, NB, 4):
        blocks = range(e, e + 4)
        rows = jnp.concatenate([sq[n] for n in blocks], axis=1)
        cols = jnp.concatenate(
            [jnp.concatenate([si[0, n], si[1, n]], axis=0) for n in blocks], axis=1
        )
        part = nt(rows, cols) * scale
        corr[...] = part if e == 0 else corr[...] + part

    for src, sem in sent:
        arrived(src, sem)
    for j in range(4):
        to_plane(j, False)
    for h in range(4):
        for y in range(2):
            ring_send(xk, R, t_s, t_r, h, y, False)
            ring_send(sq, G, g_s, g_r, h, y, False)

    def finish(g, carry):
        for f in range(2):
            e = 2 * g + f
            spread(f, e, False)
            across(f, e, False)
            share(f, e, False)
        arrived(pb.at[g], pr_s.at[g])
        return carry

    lax.fori_loop(0, 8, finish, 0)


def body(acts, grads, basis_in, basis_out):
    vmem = pl.BlockSpec(memory_space=pltpu.VMEM)
    dma = pltpu.SemaphoreType.DMA
    return pl.pallas_call(
        kernel,
        out_shape=(
            jax.ShapeDtypeStruct((A, 2 * A), F32),
            jax.ShapeDtypeStruct((G, 2 * G), F32),
            jax.ShapeDtypeStruct((G, 2 * A), F32),
        ),
        in_specs=[vmem] * 4,
        out_specs=(vmem,) * 3,
        scratch_shapes=[
            pltpu.VMEM((NB, R, B), BF16),
            pltpu.VMEM((4, Q, B), BF16),
            pltpu.VMEM((2, NB, R, B), BF16),
            pltpu.VMEM((G, 2 * G), BF16),
            pltpu.VMEM((2 * A, A), BF16),
            pltpu.VMEM((8, G, B), F32),
            pltpu.VMEM((8, G, B), BF16),
            pltpu.VMEM((8, G, B), BF16),
            pltpu.VMEM((4, G, B), F32),
            pltpu.VMEM((4, G, B), F32),
            pltpu.VMEM((NB, G, B), BF16),
            pltpu.VMEM((NB, A, B), F32),
            pltpu.VMEM((NB, A, B), F32),
            pltpu.VMEM((NB, A, B), F32),
            pltpu.VMEM((4, 4, A, B), F32),
            pltpu.VMEM((4, A, B), F32),
            pltpu.VMEM((2, NB, A, B), BF16),
            dma((3,)), dma((4,)), dma, dma((4,)), dma((NB,)), dma((NB,)),
            dma((2, NB)), dma((2, NB)), dma((NB,)), dma((NB,)), dma((NB,)), dma((NB,)),
            dma, dma, dma((2, 4, 2)), dma((2, 4, 2)), dma((8,)), dma((8,)),
            dma((2, 4)), dma((2, 4)), dma, dma, dma((2, 4, 2)), dma((2, 4, 2)),
            dma((14,)), dma((18,)),
        ],
        compiler_params=pltpu.CompilerParams(
            collective_id=0, has_side_effects=True, vmem_limit_bytes=52 << 20
        ),
        name="ekfac",
    )(acts, grads, basis_in, basis_out)


def solution(mesh):
    in_specs = (P("dp", "tile"), P("dp", "tile"), P("tile", "dp"), P("dp", "tile"))
    out_specs = (P("tile", "dp"), P("tile", "dp"), P("tile", "dp"))
    return jax.shard_map(body, mesh=mesh, in_specs=in_specs, out_specs=out_specs, check_vma=False)
```

time: 715 us -> 134 us (0.19)
  the two profiles are of different devices: /device:TPU:1 before, /device:TPU:8 now
where the time goes in v1:
time: 134 us
  Pallas kernels  127 us (95%)
  local copies, waits for them, and re-layouts  6.6 us (5%)
    pallas_call x1, Pallas kernels, body(): pl.pallas_call(kernel, out_shape=(jax.ShapeDtypeStruct((A, 2 * A), F32),...  127 us
    unnamed x9, local copies, waits for them, and re-layouts  6.6 us

profile of v1, /device:TPU:8, one launch (start us, length us, event | category | flops | bytes accessed | tf_op | source)
XLA Modules:
  0.0 134.0 jit_solution(15395026706537726509)
XLA Ops:
  0.6 0.0 copy-start
  0.6 0.0 copy-start.1
  0.7 1.0 copy.7.grads
  1.7 1.5 %copy.8.basis_out = bf16[896,448]{1,0:T(8,128)(2,1)S(1)} copy(bf16[896,448]{0,1:T(8,128)(2,1)} %param.7) | data formatting | bytes 1605632 | tf_op args[3]
  3.2 0.0 copy-done
  3.2 0.0 copy-done.1
  3.2 126.7 %ekfac.1 = (f32[128,256]{1,0:T(8,128)S(1)}, f32[448,896]{1,0:T(8,128)}, f32[448,256]{1,0:T(8,128)S(1)}) custom-call(bf16[128,128]{1,0:T(8,128)(2,1)S(1)} %copy-done.1, bf16[128,448]{1,0:T(8,128)(2,1)S(1)} %copy.7.grads, bf16[128,256]{1,0:T(8,128)(2,1)S(1)} %copy-done, bf16[896,448]{1,0:T(8,128)(2,1)S(1)} %copy.8.basis_out), custom_call_target="tpu_custom_call" | custom-call | tf_op jit(solution)/shard_map/ekfac/pallas_call | solution.py:398
  129.9 0.7 copy.12
  130.5 2.7 %copy.13 = f32[448,896]{1,0:T(8,128)} copy(f32[448,896]{1,0:T(8,128)} %get-tuple-element.7) | data formatting | bytes 3211264
  133.2 0.8 copy.14
Async XLA Ops:
  0.6 2.5 %copy-start = (bf16[128,256]{1,0:T(8,128)(2,1)S(1)}, bf16[128,256]{1,0:T(8,128)(2,1)}, u32[]{:S(2)}) copy-start(bf16[128,256]{1,0:T(8,128)(2,1)} %basis_in.1) | copy-start | bytes 196612
  0.6 2.5 %copy-start.1 = (bf16[128,128]{1,0:T(8,128)(2,1)S(1)}, bf16[128,128]{1,0:T(8,128)(2,1)}, u32[]{:S(2)}) copy-start(bf16[128,128]{1,0:T(8,128)(2,1)} %acts.1) | copy-start | bytes 98308

commit v2 on v1

v2 whole, which is shorter than its diff:
```python
import functools

import jax
import jax.numpy as jnp
from jax import lax
from jax.experimental import pallas as pl
from jax.experimental.pallas import tpu as pltpu
from jax.sharding import PartitionSpec as P

MESH = pl.DeviceIdType.MESH
F32 = jnp.float32
BF16 = jnp.bfloat16

G = 448
A = 128
R = G + A
Q = R // 4
B = 128
NB = 16
GH = G // 2
RH = R // 2

CHAIN = 2
K1, K2, K3 = 2, 4, 5
PROJECT = 3 * CHAIN + K3
STEPS = 8 + PROJECT
GATHER_AT = (3, 6, 9, 12)
REDUCE_AT = tuple(PROJECT + 1 + 2 * s for s in range(4))
INPUT_AT = (13, 15)


def mod(a, n):
    return (a + n) % n


def nt(a, b):
    return lax.dot_general(a, b, (((1,), (1,)), ((), ())), preferred_element_type=F32)


def nn(a, b):
    return lax.dot_general(a, b, (((1,), (0,)), ((), ())), preferred_element_type=F32)


def arrived(ref, sem):
    pltpu.make_async_copy(ref, ref, sem).wait()


def offset(g):
    half = (g + 1) // 2
    return 4 + half * (1 - 2 * (g % 2))


def kernel(
    acts, grads_t, basis_in, basis_out_t, act_cov, grad_out, corr,
    xk, a1, xd, bt, bit, grad_cov, pf, pb, rb, rsu, rsd, sq, pio, pis, pir, px, py, si,
    a1_s, a1_r, own_sem, d2_s, y_r, ch_s, x_s, x_r, x2_s, x2_r, c_s, c_r,
    tp_s, tp_r, t_s, t_r, pr_s, pr_r, rs_s, rs_r, gp_s, gp_r, g_s, g_r, gb_s, gb_r,
    in_s, in_r,
):
    dp, tile = lax.axis_index("dp"), lax.axis_index("tile")
    z, yl = dp // 2, dp % 2
    k, c = tile // 2, tile % 2
    x, yh = k // 4, k % 4
    up, down = mod(z + 1, 8), mod(z + 7, 8)
    partner = 2 * z + 1 - yl

    def at(z=z, yl=yl, x=x, yh=yh, c=c):
        return (2 * z + yl, (4 * x + yh) * 2 + c)

    def remote(src, dst, ss, rs, dev):
        return pltpu.make_async_remote_copy(
            src_ref=src, dst_ref=dst, send_sem=ss, recv_sem=rs, device_id=dev, device_id_type=MESH
        )

    def send(act, src, dst, ss, rs, dev):
        copy = remote(src, dst, ss, rs, dev)
        copy.start() if act else copy.wait_send()

    barrier = pltpu.get_barrier_semaphore()

    def greet(j, carry):
        pl.semaphore_signal(barrier, inc=1, device_id=(mod(dp + j, 16), tile), device_id_type=MESH)
        return carry

    lax.fori_loop(1, 16, greet, 0)
    for j in range(1, 4):
        pl.semaphore_signal(barrier, inc=1, device_id=at(x=mod(x + j, 4)), device_id_type=MESH)
        pl.semaphore_signal(barrier, inc=1, device_id=at(yh=mod(yh + j, 4)), device_id_type=MESH)
    pl.semaphore_signal(barrier, inc=1, device_id=at(c=1 - c), device_id_type=MESH)

    own_grads = pltpu.make_async_copy(grads_t, xk.at[dp, pl.ds(0, G)], own_sem.at[0])
    own_grads.start()
    weights = pltpu.make_async_copy(basis_out_t, bt, own_sem.at[1])
    weights.start()
    xk[dp, G:R] = acts[...].T
    own_grads.wait()
    pl.semaphore_wait(barrier, 22)

    def quarter(ref, q):
        return ref.at[pl.ds(pl.multiple_of(q * Q, 16), Q)]

    def over_x(act):
        for j in range(1, 4):
            q = mod(x + j, 4)
            send(act, quarter(xk.at[dp], q), a1.at[x], a1_s.at[j - 1], a1_r.at[x], at(x=q))

    over_x(True)
    keep = pltpu.make_async_copy(quarter(xk.at[dp], x), a1.at[x], own_sem.at[2])
    keep.start()
    keep.wait()

    def plane_of(col):
        return 2 * col + yh // 2, yh % 2

    def to_plane(j, act):
        col = mod(x + j, 4)
        zt, yt = plane_of(col)
        here = jnp.logical_and(zt == z, yt == yl)
        src, dst = a1.at[col], quarter(xd.at[c, dp], x)

        @pl.when(here)
        def _():
            if act:
                pltpu.make_async_copy(src, dst, y_r.at[dp]).start()

        @pl.when(jnp.logical_not(here))
        def _():
            send(act, src, dst, d2_s.at[j], y_r.at[dp], at(z=zt, yl=yt))

    for j in range(4):
        if j:
            col = mod(x + j, 4)
            arrived(a1.at[col], a1_r.at[col])
        to_plane(j, True)

    def ring_refs(buf, h, y, low, rows, far):
        zu, zd = mod(z - h, 8), mod(z + h, 8)
        if h < 3:
            a = b = pl.ds(low, rows)
        else:
            a, b = pl.ds(low, far), pl.ds(low + far, rows - far)
        return buf.at[2 * zu + y, a], buf.at[2 * zd + y, b]

    def ring_send(act, buf, s, r, h, y, p, low, rows):
        for n, ref, dev in zip((0, 1), ring_refs(buf, h, y, low, rows, rows // 2), (up, down)):
            send(act, ref, ref, s.at[n, h, p], r.at[n, h, p], at(z=dev))

    def ring_wait(buf, r, h, y, p, low, rows):
        zu, zd = mod(z - 1 - h, 8), mod(z + 1 + h, 8)
        half = rows // 2
        a = pl.ds(low, rows if h < 3 else half)
        b = pl.ds(low, rows) if h < 3 else pl.ds(low + half, half)
        arrived(buf.at[2 * zu + y, a], r.at[0, h, p])
        arrived(buf.at[2 * zd + y, b], r.at[1, h, p])

    def columns_pair(act):
        send(act, xk.at[dp], xk.at[dp], tp_s, tp_r, at(yl=1 - yl))

    def columns_send(act, h, p):
        ring_send(act, xk, t_s, t_r, h, yl if p == 0 else 1 - yl, p, 0, R)

    def columns_hop(h):
        for p in range(2):
            ring_wait(xk, t_r, h - 1, yl if p == 0 else 1 - yl, p, 0, R)
            if h < 4:
                columns_send(True, h, p)

    columns_pair(True)
    columns_send(True, 0, 0)
    bit[...] = basis_in[...].T
    weights.wait()
    arrived(xk.at[partner], tp_r)
    columns_send(True, 0, 1)

    root = 2 * (z % 2) + yl
    role = mod(yh - root, 4)
    hops = (role, mod(4 - role, 4))

    def stage(f, i, late):
        g = i - hops[f] * CHAIN - late
        e = 2 * mod(z + offset(g) + 8, 8) + f
        return jnp.logical_and(g >= 0, g < 8), e

    right, left = mod(x + 1, 4), mod(x + 3, 4)
    west, east = at(x=left), at(x=right)

    def spread(f, e, act):
        mine = quarter(xd.at[c, e], x)
        if act:
            arrived(mine, y_r.at[e])

        @pl.when(hops[f] < 3)
        def _():
            step = 1 if f == 0 else 3
            copy = remote(mine, mine, ch_s.at[e], y_r.at[e], at(yh=mod(yh + step, 4)))
            copy.start() if act else copy.wait_send()

        for n, dev in enumerate((east, west)):
            copy = remote(mine, mine, x_s.at[n, e], x_r.at[n, e], dev)
            copy.start() if act else copy.wait_send()

    def across(f, e, act):
        from_left, from_right = quarter(xd.at[c, e], left), quarter(xd.at[c, e], right)
        if act:
            arrived(from_left, x_r.at[0, e])
            arrived(from_right, x_r.at[1, e])
        ref, dev = (from_left, east) if f == 0 else (from_right, west)
        copy = remote(ref, ref, x2_s.at[e], x2_r.at[e], dev)
        copy.start() if act else copy.wait_send()

    def share(f, e, act):
        if act:
            arrived(quarter(xd.at[c, e], mod(x + 2, 4)), x2_r.at[e])
        copy = remote(xd.at[c, e], xd.at[c, e], c_s.at[e], c_r.at[e], at(c=1 - c))
        copy.start() if act else copy.wait_send()

    def pair(zz, act):
        send(act, pb.at[zz], rb.at[zz], pr_s.at[zz], pr_r.at[zz], at(yl=1 - yl))

    def project(g):
        zz = mod(z + offset(g) + 8, 8)
        cols = []
        for f in range(2):
            arrived(xd.at[1 - c, 2 * zz + f], c_r.at[2 * zz + f])
        for f in range(2):
            cols.append(jnp.concatenate([xd[0, 2 * zz + f, 0:G], xd[1, 2 * zz + f, 0:G]], axis=0))
        out = nn(bt[...], jnp.concatenate(cols, axis=1))
        first, second = out[:, 0:B], out[:, B : 2 * B]
        even = yl == 0
        pf[zz] = jnp.where(even, first, second)
        pb[zz] = jnp.where(even, second, first).astype(BF16)
        pair(zz, True)

    def total(zz):
        arrived(rb.at[zz], pr_r.at[zz])
        return pf[zz] + rb[zz].astype(F32)

    def reduce_send(act, s):
        if s == 0:
            far = mod(z + 4, 8)
            if act:
                pf[far] = total(far)
            send(act, pf.at[far, 0:GH], rsu.at[0, 0:GH], rs_s.at[0, 0], rs_r.at[0, 0], at(z=up))
            send(act, pf.at[far, GH:G], rsd.at[0, GH:G], rs_s.at[1, 0], rs_r.at[1, 0], at(z=down))
            return
        for n, (buf, zz, dev) in enumerate(
            ((rsu, mod(z + 4 - s, 8), at(z=up)), (rsd, mod(z + 4 + s, 8), at(z=down)))
        ):
            if act:
                rows = slice(0, G) if s > 1 else (slice(0, GH), slice(GH, G))[n]
                pf[zz] = total(zz)
                arrived(buf.at[s - 1, rows], rs_r.at[n, s - 1])
                pf[zz, rows] = pf[zz, rows] + buf[s - 1, rows]
            send(act, pf.at[zz], buf.at[s], rs_s.at[n, s], rs_r.at[n, s], dev)

    def project_in(act):
        if act:
            mine = bit[pl.ds(pl.multiple_of(c * A, A), A)]
            other = bit[pl.ds(pl.multiple_of((1 - c) * A, A), A)]
            for e in range(0, NB, 4):
                cols = jnp.concatenate([xk[e + n, G:R] for n in range(4)], axis=1)
                for weights, ref in ((mine, pio), (other, pis)):
                    out = nn(weights, cols)
                    for n in range(4):
                        ref[e + n] = out[:, n * B : (n + 1) * B]
        send(act, pis, pir, in_s.at[0], in_r.at[0], at(c=1 - c))

    def in_over_x(act):
        if act:
            arrived(pir, in_r.at[0])
            pio[...] = pio[...] + pir[...]
        for j in range(1, 4):
            q = mod(x + j, 4)
            send(act, pio.at[pl.ds(4 * q, 4)], px.at[x], in_s.at[j], in_r.at[1 + x], at(x=q))

    def in_over_y(act):
        mine = pl.ds(4 * x, 4)
        if act:
            acc = pio[mine]
            for j in range(1, 4):
                q = mod(x + j, 4)
                arrived(px.at[q], in_r.at[1 + q])
                acc = acc + px[q]
            pio[mine] = acc
        for j in range(1, 4):
            w = mod(yh + j, 4)
            send(act, pio.at[4 * x + w], py.at[yh], in_s.at[3 + j], in_r.at[5 + yh], at(yh=w))

    def in_square(act):
        if act:
            acc = pio[k]
            for j in range(1, 4):
                w = mod(yh + j, 4)
                arrived(py.at[w], in_r.at[5 + w])
                acc = acc + py[w]
            si[c, k] = (acc * acc).astype(BF16)
        for j in range(1, 4):
            w = mod(yh + j, 4)
            send(act, si.at[c, k], si.at[c, k], in_s.at[6 + j], in_r.at[9 + yh], at(yh=w))

    def in_gather_x(act):
        if act:
            for j in range(1, 4):
                w = mod(yh + j, 4)
                arrived(si.at[c, 4 * x + w], in_r.at[9 + w])
        mine = si.at[c, pl.ds(4 * x, 4)]
        for j in range(1, 4):
            q = mod(x + j, 4)
            send(act, mine, mine, in_s.at[9 + j], in_r.at[13 + x], at(x=q))

    def in_share(act):
        if act:
            for j in range(1, 4):
                q = mod(x + j, 4)
                arrived(si.at[c, pl.ds(4 * q, 4)], in_r.at[13 + q])
        send(act, si.at[c], si.at[c], in_s.at[13], in_r.at[17], at(c=1 - c))

    def squares_send(act, h, p):
        if p == 0:
            ring_send(act, sq, g_s, g_r, h, yl, 0, 0, G)
        else:
            ring_send(act, sq, g_s, g_r, h, 1 - yl, 1, 0, GH)

    def lower(act, zz):
        ref = sq.at[2 * zz + yl, GH:G]
        send(act, ref, ref, gb_s.at[zz], gb_r.at[zz], at(yl=1 - yl))

    def upper(act):
        ref = sq.at[dp, 0:GH]
        send(act, ref, ref, gp_s, gp_r, at(yl=1 - yl))

    def squares_hop(h):
        ring_wait(sq, g_r, h - 1, yl, 0, 0, G)
        if h < 4:
            squares_send(True, h, 0)
        for zz in (mod(z - h, 8), mod(z + h, 8))[: 2 if h < 4 else 1]:
            lower(True, zz)
        ring_wait(sq, g_r, h - 1, 1 - yl, 1, 0, GH)
        if h < 4:
            squares_send(True, h, 1)

    scale = 1.0 / (NB * B)

    def covariances(first):
        for e in (first, first + 4):
            blocks = range(e, e + 4)
            rows = jnp.concatenate([xk[n, 0:G] for n in blocks], axis=1)
            cols = jnp.concatenate(
                [jnp.concatenate([xd[0, n, 0:G], xd[1, n, 0:G]], axis=0) for n in blocks], axis=1
            )
            part = nt(rows, cols) * scale
            grad_cov[...] = part if e == 0 else grad_cov[...] + part
            rows = jnp.concatenate([xk[n, G:R] for n in blocks], axis=1)
            cols = jnp.concatenate(
                [jnp.concatenate([xd[0, n, G:R], xd[1, n, G:R]], axis=0) for n in blocks], axis=1
            )
            part = nt(rows, cols) * scale
            act_cov[...] = part if e == 0 else act_cov[...] + part

    def store(act):
        copy = pltpu.make_async_copy(grad_cov, grad_out, own_sem.at[3])
        copy.start() if act else copy.wait()

    work = {}
    for n, when in enumerate(GATHER_AT):
        work.setdefault(when, []).append(functools.partial(columns_hop, n + 1))
    for n, when in enumerate(REDUCE_AT):
        work.setdefault(when, []).append(functools.partial(reduce_send, True, n))
    for when, fn in zip(INPUT_AT, (project_in, in_over_x)):
        work.setdefault(when, []).append(functools.partial(fn, True))

    def step(i, carry):
        for f in range(2):
            for late, fn in ((0, spread), (K1, across), (K2, share)):
                valid, e = stage(f, i, late)

                @pl.when(valid)
                def _():
                    fn(f, e, True)

        g = i - PROJECT

        @pl.when(jnp.logical_and(g >= 0, g < 8))
        def _():
            project(g)

        for when in sorted(work):
            if when < STEPS:

                @pl.when(i == when)
                def _():
                    for fn in work[when]:
                        fn()

        return carry

    lax.fori_loop(0, STEPS, step, 0)
    for when in sorted(work):
        if when >= STEPS:
            for fn in work[when]:
                fn()

    covariances(0)
    in_over_y(True)

    arrived(rsu.at[3], rs_r.at[0, 3])
    arrived(rsd.at[3], rs_r.at[1, 3])
    mine = total(z) + rsu[3] + rsd[3]
    sq[dp] = (mine * mine).astype(BF16)

    upper(True)
    squares_send(True, 0, 0)
    lower(True, z)
    arrived(sq.at[partner, 0:GH], gp_r)
    squares_send(True, 0, 1)
    in_square(True)
    squares_hop(1)
    in_gather_x(True)
    covariances(8)
    store(True)
    squares_hop(2)
    in_share(True)
    squares_hop(3)
    arrived(si.at[1 - c], in_r.at[17])
    squares_hop(4)
    for zz in range(8):
        arrived(sq.at[2 * zz + 1 - yl, GH:G], gb_r.at[zz])

    for e in range(0, NB, 4):
        blocks = range(e, e + 4)
        rows = jnp.concatenate([sq[n] for n in blocks], axis=1)
        cols = jnp.concatenate(
            [jnp.concatenate([si[0, n], si[1, n]], axis=0) for n in blocks], axis=1
        )
        part = nt(rows, cols) * scale
        corr[...] = part if e == 0 else corr[...] + part

    store(False)
    over_x(False)
    for j in range(4):
        to_plane(j, False)
    columns_pair(False)
    upper(False)
    for h in range(4):
        reduce_send(False, h)
        for p in range(2):
            columns_send(False, h, p)
            squares_send(False, h, p)
    for fn in (project_in, in_over_x, in_over_y, in_square, in_gather_x, in_share):
        fn(False)

    def finish(g, carry):
        for f in range(2):
            e = 2 * g + f
            spread(f, e, False)
            across(f, e, False)
            share(f, e, False)
        pair(g, False)
        lower(False, g)
        return carry

    lax.fori_loop(0, 8, finish, 0)


def body(acts, grads, basis_in, basis_out):
    vmem = pl.BlockSpec(memory_space=pltpu.VMEM)
    hbm = pl.BlockSpec(memory_space=pltpu.HBM)
    dma = pltpu.SemaphoreType.DMA
    shapes = (
        jax.ShapeDtypeStruct((A, 2 * A), F32),
        jax.ShapeDtypeStruct((G, 2 * G), F32),
        jax.ShapeDtypeStruct((G, 2 * A), F32),
    )
    return pl.pallas_call(
        kernel,
        out_shape=shapes,
        in_specs=[vmem, hbm, vmem, hbm],
        out_specs=(vmem, hbm, vmem),
        scratch_shapes=[
            pltpu.VMEM((NB, R, B), BF16),
            pltpu.VMEM((4, Q, B), BF16),
            pltpu.VMEM((2, NB, R, B), BF16),
            pltpu.VMEM((G, 2 * G), BF16),
            pltpu.VMEM((2 * A, A), BF16),
            pltpu.VMEM((G, 2 * G), F32),
            pltpu.VMEM((8, G, B), F32),
            pltpu.VMEM((8, G, B), BF16),
            pltpu.VMEM((8, G, B), BF16),
            pltpu.VMEM((4, G, B), F32),
            pltpu.VMEM((4, G, B), F32),
            pltpu.VMEM((NB, G, B), BF16),
            pltpu.VMEM((NB, A, B), F32),
            pltpu.VMEM((NB, A, B), F32),
            pltpu.VMEM((NB, A, B), F32),
            pltpu.VMEM((4, 4, A, B), F32),
            pltpu.VMEM((4, A, B), F32),
            pltpu.VMEM((2, NB, A, B), BF16),
            dma((3,)), dma((4,)), dma((4,)), dma((4,)), dma((NB,)), dma((NB,)),
            dma((2, NB)), dma((2, NB)), dma((NB,)), dma((NB,)), dma((NB,)), dma((NB,)),
            dma, dma, dma((2, 4, 2)), dma((2, 4, 2)), dma((8,)), dma((8,)),
            dma((2, 4)), dma((2, 4)), dma, dma, dma((2, 4, 2)), dma((2, 4, 2)), dma((8,)), dma((8,)),
            dma((14,)), dma((18,)),
        ],
        compiler_params=pltpu.CompilerParams(
            collective_id=0, has_side_effects=True, vmem_limit_bytes=62 << 20
        ),
        name="ekfac",
    )(acts, grads.T, basis_in, basis_out.T)


def solution(mesh):
    in_specs = (P("dp", "tile"), P("dp", "tile"), P("tile", "dp"), P("dp", "tile"))
    out_specs = (P("tile", "dp"), P("tile", "dp"), P("tile", "dp"))
    return jax.shard_map(body, mesh=mesh, in_specs=in_specs, out_specs=out_specs, check_vma=False)
```

time: 134 us -> 115 us (0.86)
  the two profiles are of different devices: /device:TPU:8 before, /device:TPU:1 now
where the time goes in v2:
time: 115 us; the launch traced here: 113 us
  Pallas kernels  107 us (93%)
  local copies, waits for them, and re-layouts  5.07 us (4%)
    pallas_call x1, Pallas kernels, body(): pl.pallas_call(kernel, out_shape=shapes, in_specs=[vmem, hbm, vmem, hbm],...  107 us
    unnamed x5, local copies, waits for them, and re-layouts  5.07 us

profile of v2, /device:TPU:1, one launch (start us, length us, event | category | flops | bytes accessed | tf_op | source)
XLA Modules:
  0.0 113.1 jit_solution(4762345567686427160)
XLA Ops:
  0.6 107.4 %ekfac.1 = (f32[128,256]{1,0:T(8,128)}, f32[448,896]{1,0:T(8,128)}, f32[448,256]{1,0:T(8,128)}) custom-call(bf16[128,128]{1,0:T(8,128)(2,1)} %acts.1, bf16[448,128]{1,0:T(8,128)(2,1)} %bitcast.3, bf16[128,256]{1,0:T(8,128)(2,1)} %basis_in.1, bf16[448,896]{1,0:T(8,128)(2,1)} %bitcast.2), custom_call_target="tpu_custom_call" | custom-call | tf_op jit(solution)/shard_map/ekfac/pallas_call | solution.py:474
  108.0 1.6 %copy.10 = f32[128,256]{1,0:T(8,128)} copy(f32[128,256]{1,0:T(8,128)} %get-tuple-element.6) | data formatting | bytes 262144
  109.6 0.0 copy-start
  109.6 2.7 %copy.11 = f32[448,896]{1,0:T(8,128)} copy(f32[448,896]{1,0:T(8,128)} %get-tuple-element.7) | data formatting | bytes 3211264
  112.3 0.0 copy-done
  112.3 0.8 copy.12
Async XLA Ops:
  109.6 2.7 %copy-start = (f32[448,256]{1,0:T(8,128)S(1)}, f32[448,256]{1,0:T(8,128)}, u32[]{:S(2)}) copy-start(f32[448,256]{1,0:T(8,128)} %get-tuple-element.8) | copy-start | bytes 1376260

commit v3 on v2

--- a/solution.py
+++ b/solution.py
@@ -18,14 +18,14 @@
 B = 128
 NB = 16
 GH = G // 2
-RH = R // 2
+GQ = G // 4
 
 CHAIN = 2
 K1, K2, K3 = 2, 4, 5
 PROJECT = 3 * CHAIN + K3
 STEPS = 8 + PROJECT
 GATHER_AT = (3, 6, 9, 12)
-REDUCE_AT = tuple(PROJECT + 1 + 2 * s for s in range(4))
+REDUCE_AT = PROJECT + 1
 INPUT_AT = (13, 15)
 
 
@@ -133,35 +133,44 @@
             arrived(a1.at[col], a1_r.at[col])
         to_plane(j, True)
 
-    def ring_refs(buf, h, y, low, rows, far):
-        zu, zd = mod(z - h, 8), mod(z + h, 8)
+    def columns_rows(n, h, p):
         if h < 3:
-            a = b = pl.ds(low, rows)
-        else:
-            a, b = pl.ds(low, far), pl.ds(low + far, rows - far)
-        return buf.at[2 * zu + y, a], buf.at[2 * zd + y, b]
-
-    def ring_send(act, buf, s, r, h, y, p, low, rows):
-        for n, ref, dev in zip((0, 1), ring_refs(buf, h, y, low, rows, rows // 2), (up, down)):
-            send(act, ref, ref, s.at[n, h, p], r.at[n, h, p], at(z=dev))
-
-    def ring_wait(buf, r, h, y, p, low, rows):
-        zu, zd = mod(z - 1 - h, 8), mod(z + 1 + h, 8)
-        half = rows // 2
-        a = pl.ds(low, rows if h < 3 else half)
-        b = pl.ds(low, rows) if h < 3 else pl.ds(low + half, half)
-        arrived(buf.at[2 * zu + y, a], r.at[0, h, p])
-        arrived(buf.at[2 * zd + y, b], r.at[1, h, p])
+            return pl.ds(0, R)
+        return pl.ds(n * (R // 2), R // 2)
+
+    def squares_rows(n, h, p):
+        if h < 3:
+            return pl.ds(GH, GH) if p == 0 else pl.ds(0, GH)
+        if p == 2:
+            return pl.ds(n * GQ, GQ)
+        return (None if n == 0 else pl.ds(GH, GH)) if p == 0 else (pl.ds(0, GH) if n == 0 else None)
+
+    def ring_ref(buf, rows, n, h, p, y, shift):
+        zz = mod(z - shift - h, 8) if n == 0 else mod(z + shift + h, 8)
+        part = rows(n, h, p)
+        return None if part is None else buf.at[2 * zz + y, part]
+
+    def ring_send(act, buf, rows, s, r, h, p, y):
+        for n, dev in ((0, up), (1, down)):
+            ref = ring_ref(buf, rows, n, h, p, y, 0)
+            if ref is not None:
+                send(act, ref, ref, s.at[n, h, p], r.at[n, h, p], at(z=dev))
+
+    def ring_wait(buf, rows, r, h, p, y):
+        for n in range(2):
+            ref = ring_ref(buf, rows, n, h, p, y, 1)
+            if ref is not None:
+                arrived(ref, r.at[n, h, p])
 
     def columns_pair(act):
         send(act, xk.at[dp], xk.at[dp], tp_s, tp_r, at(yl=1 - yl))
 
     def columns_send(act, h, p):
-        ring_send(act, xk, t_s, t_r, h, yl if p == 0 else 1 - yl, p, 0, R)
+        ring_send(act, xk, columns_rows, t_s, t_r, h, p, yl if p == 0 else 1 - yl)
 
     def columns_hop(h):
         for p in range(2):
-            ring_wait(xk, t_r, h - 1, yl if p == 0 else 1 - yl, p, 0, R)
+            ring_wait(xk, columns_rows, t_r, h - 1, p, yl if p == 0 else 1 - yl)
             if h < 4:
                 columns_send(True, h, p)
 
@@ -231,27 +240,33 @@
         pb[zz] = jnp.where(even, second, first).astype(BF16)
         pair(zz, True)
 
-    def total(zz):
-        arrived(rb.at[zz], pr_r.at[zz])
-        return pf[zz] + rb[zz].astype(F32)
-
-    def reduce_send(act, s):
-        if s == 0:
-            far = mod(z + 4, 8)
+    def reduce_send(act, s, j):
+        for n, (buf, sign, dev) in enumerate(((rsu, -s, up), (rsd, s, down))):
+            zz = mod(z + 4 + sign, 8)
+            if s == 0:
+                part = j + 2 * n
+            else:
+                part = (j + 2) % 4 if n == 0 else j
+            rows = slice(part * GQ, part * GQ + GQ)
             if act:
-                pf[far] = total(far)
-            send(act, pf.at[far, 0:GH], rsu.at[0, 0:GH], rs_s.at[0, 0], rs_r.at[0, 0], at(z=up))
-            send(act, pf.at[far, GH:G], rsd.at[0, GH:G], rs_s.at[1, 0], rs_r.at[1, 0], at(z=down))
-            return
-        for n, (buf, zz, dev) in enumerate(
-            ((rsu, mod(z + 4 - s, 8), at(z=up)), (rsd, mod(z + 4 + s, 8), at(z=down)))
-        ):
-            if act:
-                rows = slice(0, G) if s > 1 else (slice(0, GH), slice(GH, G))[n]
-                pf[zz] = total(zz)
-                arrived(buf.at[s - 1, rows], rs_r.at[n, s - 1])
-                pf[zz, rows] = pf[zz, rows] + buf[s - 1, rows]
-            send(act, pf.at[zz], buf.at[s], rs_s.at[n, s], rs_r.at[n, s], dev)
+                if j == 0 and (s > 0 or n == 0):
+                    arrived(rb.at[zz], pr_r.at[zz])
+                value = pf[zz, rows] + rb[zz, rows].astype(F32)
+                if s > 1 or (s == 1 and part // 2 == n):
+                    arrived(buf.at[s - 1, rows], rs_r.at[n, s - 1, part])
+                    value = value + buf[s - 1, rows]
+                pf[zz, rows] = value
+            send(act, pf.at[zz, rows], buf.at[s, rows], rs_s.at[n, s, part], rs_r.at[n, s, part], at(z=dev))
+
+    def reduce_end():
+        arrived(rb.at[z], pr_r.at[z])
+        for part in (0, 2, 1, 3):
+            rows = slice(part * GQ, part * GQ + GQ)
+            value = pf[z, rows] + rb[z, rows].astype(F32)
+            for n, buf in enumerate((rsu, rsd)):
+                arrived(buf.at[3, rows], rs_r.at[n, 3, part])
+                value = value + buf[3, rows]
+            sq[dp, rows] = (value * value).astype(BF16)
 
     def project_in(act):
         if act:
@@ -316,10 +331,7 @@
         send(act, si.at[c], si.at[c], in_s.at[13], in_r.at[17], at(c=1 - c))
 
     def squares_send(act, h, p):
-        if p == 0:
-            ring_send(act, sq, g_s, g_r, h, yl, 0, 0, G)
-        else:
-            ring_send(act, sq, g_s, g_r, h, 1 - yl, 1, 0, GH)
+        ring_send(act, sq, squares_rows, g_s, g_r, h, p, yl if p < 2 else 1 - yl)
 
     def lower(act, zz):
         ref = sq.at[2 * zz + yl, GH:G]
@@ -330,14 +342,13 @@
         send(act, ref, ref, gp_s, gp_r, at(yl=1 - yl))
 
     def squares_hop(h):
-        ring_wait(sq, g_r, h - 1, yl, 0, 0, G)
-        if h < 4:
-            squares_send(True, h, 0)
-        for zz in (mod(z - h, 8), mod(z + h, 8))[: 2 if h < 4 else 1]:
-            lower(True, zz)
-        ring_wait(sq, g_r, h - 1, 1 - yl, 1, 0, GH)
-        if h < 4:
-            squares_send(True, h, 1)
+        for p in range(3):
+            ring_wait(sq, squares_rows, g_r, h - 1, p, yl if p < 2 else 1 - yl)
+            if h < 4:
+                squares_send(True, h, p)
+            if p == 0:
+                for zz in (mod(z - h, 8), mod(z + h, 8))[: 2 if h < 4 else 1]:
+                    lower(True, zz)
 
     scale = 1.0 / (NB * B)
 
@@ -357,6 +368,16 @@
             part = nt(rows, cols) * scale
             act_cov[...] = part if e == 0 else act_cov[...] + part
 
+    def correct(distances):
+        places = [mod(z + n, 8) for n in distances]
+        for zz in places:
+            arrived(sq.at[2 * zz + 1 - yl, GH:G], gb_r.at[zz])
+        blocks = [2 * zz + y for zz in places for y in range(2)]
+        rows = jnp.concatenate([sq[e] for e in blocks], axis=1)
+        cols = jnp.concatenate([jnp.concatenate([si[0, e], si[1, e]], axis=0) for e in blocks], axis=1)
+        part = nt(rows, cols) * scale
+        corr[...] = part if 0 in distances else corr[...] + part
+
     def store(act):
         copy = pltpu.make_async_copy(grad_cov, grad_out, own_sem.at[3])
         copy.start() if act else copy.wait()
@@ -364,8 +385,10 @@
     work = {}
     for n, when in enumerate(GATHER_AT):
         work.setdefault(when, []).append(functools.partial(columns_hop, n + 1))
-    for n, when in enumerate(REDUCE_AT):
-        work.setdefault(when, []).append(functools.partial(reduce_send, True, n))
+    for n in range(4):
+        for j in range(2 if n == 0 else 4):
+            when = REDUCE_AT + 2 * n + (0 if n == 0 else j // 2)
+            work.setdefault(when, []).append(functools.partial(reduce_send, True, n, j))
     for when, fn in zip(INPUT_AT, (project_in, in_over_x)):
         work.setdefault(when, []).append(functools.partial(fn, True))
 
@@ -403,16 +426,13 @@
     covariances(0)
     in_over_y(True)
 
-    arrived(rsu.at[3], rs_r.at[0, 3])
-    arrived(rsd.at[3], rs_r.at[1, 3])
-    mine = total(z) + rsu[3] + rsd[3]
-    sq[dp] = (mine * mine).astype(BF16)
-
+    reduce_end()
     upper(True)
     squares_send(True, 0, 0)
+    squares_send(True, 0, 1)
     lower(True, z)
     arrived(sq.at[partner, 0:GH], gp_r)
-    squares_send(True, 0, 1)
+    squares_send(True, 0, 2)
     in_square(True)
     squares_hop(1)
     in_gather_x(True)
@@ -422,18 +442,9 @@
     in_share(True)
     squares_hop(3)
     arrived(si.at[1 - c], in_r.at[17])
+    correct((0, 1, 7, 2, 6))
     squares_hop(4)
-    for zz in range(8):
-        arrived(sq.at[2 * zz + 1 - yl, GH:G], gb_r.at[zz])
-
-    for e in range(0, NB, 4):
-        blocks = range(e, e + 4)
-        rows = jnp.concatenate([sq[n] for n in blocks], axis=1)
-        cols = jnp.concatenate(
-            [jnp.concatenate([si[0, n], si[1, n]], axis=0) for n in blocks], axis=1
-        )
-        part = nt(rows, cols) * scale
-        corr[...] = part if e == 0 else corr[...] + part
+    correct((3, 5, 4))
 
     store(False)
     over_x(False)
@@ -442,9 +453,11 @@
     columns_pair(False)
     upper(False)
     for h in range(4):
-        reduce_send(False, h)
+        for j in range(2 if h == 0 else 4):
+            reduce_send(False, h, j)
         for p in range(2):
             columns_send(False, h, p)
+        for p in range(3):
             squares_send(False, h, p)
     for fn in (project_in, in_over_x, in_over_y, in_square, in_gather_x, in_share):
         fn(False)
@@ -462,6 +475,28 @@
     lax.fori_loop(0, 8, finish, 0)
 
 
+def settle(*refs):
+    ins, outs, held, sems = refs[0:3], refs[3:6], refs[6:9], refs[9]
+    steps = []
+    for n, parts in ((1, 4), (2, 2), (0, 1)):
+        rows = ins[n].shape[0] // parts
+        for j in range(parts):
+            at, m = pl.ds(j * rows, rows), len(steps)
+            steps.append(
+                (
+                    pltpu.make_async_copy(ins[n].at[at], held[n].at[at], sems.at[0, m]),
+                    pltpu.make_async_copy(held[n].at[at], outs[n].at[at], sems.at[1, m]),
+                )
+            )
+    for read, _ in steps:
+        read.start()
+    for read, write in steps:
+        read.wait()
+        write.start()
+    for _, write in steps:
+        write.wait()
+
+
 def body(acts, grads, basis_in, basis_out):
     vmem = pl.BlockSpec(memory_space=pltpu.VMEM)
     hbm = pl.BlockSpec(memory_space=pltpu.HBM)
@@ -471,7 +506,7 @@
         jax.ShapeDtypeStruct((G, 2 * G), F32),
         jax.ShapeDtypeStruct((G, 2 * A), F32),
     )
-    return pl.pallas_call(
+    results = pl.pallas_call(
         kernel,
         out_shape=shapes,
         in_specs=[vmem, hbm, vmem, hbm],
@@ -498,7 +533,7 @@
             dma((3,)), dma((4,)), dma((4,)), dma((4,)), dma((NB,)), dma((NB,)),
             dma((2, NB)), dma((2, NB)), dma((NB,)), dma((NB,)), dma((NB,)), dma((NB,)),
             dma, dma, dma((2, 4, 2)), dma((2, 4, 2)), dma((8,)), dma((8,)),
-            dma((2, 4)), dma((2, 4)), dma, dma, dma((2, 4, 2)), dma((2, 4, 2)), dma((8,)), dma((8,)),
+            dma((2, 4, 4)), dma((2, 4, 4)), dma, dma, dma((2, 4, 3)), dma((2, 4, 3)), dma((8,)), dma((8,)),
             dma((14,)), dma((18,)),
         ],
         compiler_params=pltpu.CompilerParams(
@@ -506,6 +541,15 @@
         ),
         name="ekfac",
     )(acts, grads.T, basis_in, basis_out.T)
+    return pl.pallas_call(
+        settle,
+        out_shape=shapes,
+        in_specs=[hbm] * 3,
+        out_specs=(hbm,) * 3,
+        scratch_shapes=[pltpu.VMEM(shape.shape, F32) for shape in shapes] + [dma((2, 8))],
+        compiler_params=pltpu.CompilerParams(vmem_limit_bytes=62 << 20),
+        name="settle",
+    )(*results)
 
 
 def solution(mesh):

time: 115 us -> 111 us (0.965)
  local copies, waits for them, and re-layouts: 5.07 us -> 0 us
  Pallas kernels: 107 us -> 110 us
    unnamed x5 -> x0, local copies, waits for them, and re-layouts: 5.07 us -> none
    pallas_call x0 -> x1, Pallas kernels: none -> 2.47 us  [body(): pl.pallas_call(settle, out_shape=shapes, in_specs=[hbm] * 3, out_specs=(h...]
where the time goes in v3:
time: 111 us; the launch traced here: 110 us
  Pallas kernels  110 us (99%)
    pallas_call x1, Pallas kernels, body(): pl.pallas_call(kernel, out_shape=shapes, in_specs=[vmem, hbm, vmem, hbm],...  107 us
    pallas_call x1, Pallas kernels, body(): pl.pallas_call(settle, out_shape=shapes, in_specs=[hbm] * 3, out_specs=(h...  2.47 us

profile of v3, /device:TPU:1, one launch (start us, length us, event | category | flops | bytes accessed | tf_op | source)
XLA Modules:
  0.0 110.2 jit_solution(6370844334601913355)
XLA Ops:
  0.6 107.1 %ekfac.1 = (f32[128,256]{1,0:T(8,128)}, f32[448,896]{1,0:T(8,128)}, f32[448,256]{1,0:T(8,128)}) custom-call(bf16[128,128]{1,0:T(8,128)(2,1)} %acts.1, bf16[448,128]{1,0:T(8,128)(2,1)} %bitcast.3, bf16[128,256]{1,0:T(8,128)(2,1)} %basis_in.1, bf16[448,896]{1,0:T(8,128)(2,1)} %bitcast.2), custom_call_target="tpu_custom_call" | custom-call | tf_op jit(solution)/shard_map/ekfac/pallas_call | solution.py:509
  107.7 2.5 %settle.1 = (f32[128,256]{1,0:T(8,128)}, f32[448,896]{1,0:T(8,128)}, f32[448,256]{1,0:T(8,128)}) custom-call(f32[128,256]{1,0:T(8,128)} %get-tuple-element.6.refs_0_, f32[448,896]{1,0:T(8,128)} %get-tuple-element.7.refs_1_, f32[448,256]{1,0:T(8,128)} %get-tuple-element.8.refs_2_), custom_call_target="tpu_custom_call" | custom-call | tf_op jit(solution)/shard_map/settle/pallas_call | solution.py:544

commit v4 on v3

--- a/solution.py
+++ b/solution.py
@@ -14,7 +14,8 @@
 G = 448
 A = 128
 R = G + A
-Q = R // 4
+Q = G // 4
+U = A // 4
 B = 128
 NB = 16
 GH = G // 2
@@ -26,6 +27,7 @@
 STEPS = 8 + PROJECT
 GATHER_AT = (3, 6, 9, 12)
 REDUCE_AT = PROJECT + 1
+ACTS_AT = 12
 INPUT_AT = (13, 15)
 
 
@@ -52,8 +54,8 @@
 
 def kernel(
     acts, grads_t, basis_in, basis_out_t, act_cov, grad_out, corr,
-    xk, a1, xd, bt, bit, grad_cov, pf, pb, rb, rsu, rsd, sq, pio, pis, pir, px, py, si,
-    a1_s, a1_r, own_sem, d2_s, y_r, ch_s, x_s, x_r, x2_s, x2_r, c_s, c_r,
+    xk, a1, aa, xd, bt, bit, grad_cov, pf, pb, rb, rsu, rsd, sq, pio, pis, pir, px, py, si,
+    a1_s, a1_r, aa_s, aa_r, own_sem, d2_s, da_s, y_r, ya_r, yb_s, yb_r, xa_s, xa_r, xb_s, xb_r, ca_s, ca_r, ch_s, x_s, x_r, x2_s, x2_r, c_s, c_r,
     tp_s, tp_r, t_s, t_r, pr_s, pr_r, rs_s, rs_r, gp_s, gp_r, g_s, g_r, gb_s, gb_r,
     in_s, in_r,
 ):
@@ -99,6 +101,9 @@
     def quarter(ref, q):
         return ref.at[pl.ds(pl.multiple_of(q * Q, 16), Q)]
 
+    def acts_quarter(ref, q):
+        return ref.at[pl.ds(pl.multiple_of(G + q * U, 16), U)]
+
     def over_x(act):
         for j in range(1, 4):
             q = mod(x + j, 4)
@@ -109,29 +114,50 @@
     keep.start()
     keep.wait()
 
+    def acts_over_x(act):
+        for j in range(1, 4):
+            q = mod(x + j, 4)
+            send(act, acts_quarter(xk.at[dp], q), aa.at[x], aa_s.at[j - 1], aa_r.at[x], at(x=q))
+        if act:
+            copy = pltpu.make_async_copy(acts_quarter(xk.at[dp], x), aa.at[x], own_sem.at[4])
+            copy.start()
+            copy.wait()
+
     def plane_of(col):
         return 2 * col + yh // 2, yh % 2
 
-    def to_plane(j, act):
+    def to_plane(j, act, whose=0):
         col = mod(x + j, 4)
         zt, yt = plane_of(col)
         here = jnp.logical_and(zt == z, yt == yl)
-        src, dst = a1.at[col], quarter(xd.at[c, dp], x)
+        place = xd.at[c, yl, z]
+        if whose == 0:
+            src, dst, ss, rs = a1.at[col], quarter(place, x), d2_s.at[j], y_r.at[dp]
+        else:
+            src, dst, ss, rs = aa.at[col], acts_quarter(place, x), da_s.at[j], ya_r.at[dp]
 
         @pl.when(here)
         def _():
             if act:
-                pltpu.make_async_copy(src, dst, y_r.at[dp]).start()
+                pltpu.make_async_copy(src, dst, rs).start()
 
         @pl.when(jnp.logical_not(here))
         def _():
-            send(act, src, dst, d2_s.at[j], y_r.at[dp], at(z=zt, yl=yt))
+            send(act, src, dst, ss, rs, at(z=zt, yl=yt))
 
     for j in range(4):
         if j:
             col = mod(x + j, 4)
             arrived(a1.at[col], a1_r.at[col])
         to_plane(j, True)
+
+    def acts_to_planes():
+        for j in range(4):
+            if j:
+                col = mod(x + j, 4)
+                arrived(aa.at[col], aa_r.at[col])
+            to_plane(j, True, 1)
+
 
     def columns_rows(n, h, p):
         if h < 3:
@@ -194,7 +220,7 @@
     west, east = at(x=left), at(x=right)
 
     def spread(f, e, act):
-        mine = quarter(xd.at[c, e], x)
+        mine = quarter(xd.at[c, f, e // 2], x)
         if act:
             arrived(mine, y_r.at[e])
 
@@ -209,7 +235,7 @@
             copy.start() if act else copy.wait_send()
 
     def across(f, e, act):
-        from_left, from_right = quarter(xd.at[c, e], left), quarter(xd.at[c, e], right)
+        from_left, from_right = quarter(xd.at[c, f, e // 2], left), quarter(xd.at[c, f, e // 2], right)
         if act:
             arrived(from_left, x_r.at[0, e])
             arrived(from_right, x_r.at[1, e])
@@ -219,20 +245,58 @@
 
     def share(f, e, act):
         if act:
-            arrived(quarter(xd.at[c, e], mod(x + 2, 4)), x2_r.at[e])
-        copy = remote(xd.at[c, e], xd.at[c, e], c_s.at[e], c_r.at[e], at(c=1 - c))
-        copy.start() if act else copy.wait_send()
+            arrived(quarter(xd.at[c, f, e // 2], mod(x + 2, 4)), x2_r.at[e])
+        ref = xd.at[c, f, e // 2, pl.ds(0, G)]
+        send(act, ref, ref, c_s.at[e], c_r.at[e], at(c=1 - c))
 
     def pair(zz, act):
         send(act, pb.at[zz], rb.at[zz], pr_s.at[zz], pr_r.at[zz], at(yl=1 - yl))
+
+    def acts_ref(f, q):
+        return xd.at[c, f, pl.ds(0, 8), pl.ds(pl.multiple_of(G + q * U, 16), U)]
+
+    def acts_spread(f, act):
+        ref = acts_ref(f, x)
+        if act:
+
+            @pl.when(role == 0)
+            def _():
+                for zz in range(8):
+                    arrived(xd.at[c, f, zz, pl.ds(G, U)], ya_r.at[2 * zz + f])
+
+            @pl.when(role != 0)
+            def _():
+                arrived(ref, yb_r.at[f])
+
+        @pl.when(hops[f] < 3)
+        def _():
+            send(act, ref, ref, yb_s.at[f], yb_r.at[f], at(yh=mod(yh + (1 if f == 0 else 3), 4)))
+
+        for n, dev in enumerate((east, west)):
+            send(act, ref, ref, xa_s.at[n, f], xa_r.at[n, f], dev)
+
+    def acts_across(act):
+        for f in range(2):
+            if act:
+                arrived(acts_ref(f, left), xa_r.at[0, f])
+                arrived(acts_ref(f, right), xa_r.at[1, f])
+            ref, dev = (acts_ref(f, left), east) if f == 0 else (acts_ref(f, right), west)
+            send(act, ref, ref, xb_s.at[f], xb_r.at[f], dev)
+
+    def acts_share(act):
+        for f in range(2):
+            if act:
+                arrived(acts_ref(f, mod(x + 2, 4)), xb_r.at[f])
+            ref = xd.at[c, f, pl.ds(0, 8), pl.ds(G, A)]
+            send(act, ref, ref, ca_s.at[f], ca_r.at[f], at(c=1 - c))
 
     def project(g):
         zz = mod(z + offset(g) + 8, 8)
         cols = []
         for f in range(2):
-            arrived(xd.at[1 - c, 2 * zz + f], c_r.at[2 * zz + f])
+            arrived(xd.at[1 - c, f, zz, pl.ds(0, G)], c_r.at[2 * zz + f])
         for f in range(2):
-            cols.append(jnp.concatenate([xd[0, 2 * zz + f, 0:G], xd[1, 2 * zz + f, 0:G]], axis=0))
+            cols.append(jnp.concatenate([xd[0, f, zz, 0:G], xd[1, f, zz, 0:G]], axis=0))
         out = nn(bt[...], jnp.concatenate(cols, axis=1))
         first, second = out[:, 0:B], out[:, B : 2 * B]
         even = yl == 0
@@ -352,21 +416,27 @@
 
     scale = 1.0 / (NB * B)
 
+    def covariance(out, low, high, blocks):
+        rows = jnp.concatenate([xk[e, low:high] for e in blocks], axis=1)
+        cols = jnp.concatenate(
+            [
+                jnp.concatenate([xd[n, e % 2, e // 2, low:high] for n in range(2)], axis=0)
+                for e in blocks
+            ],
+            axis=1,
+        )
+        part = nt(rows, cols) * scale
+        out[...] = part if 0 in blocks else out[...] + part
+
     def covariances(first):
         for e in (first, first + 4):
-            blocks = range(e, e + 4)
-            rows = jnp.concatenate([xk[n, 0:G] for n in blocks], axis=1)
-            cols = jnp.concatenate(
-                [jnp.concatenate([xd[0, n, 0:G], xd[1, n, 0:G]], axis=0) for n in blocks], axis=1
-            )
-            part = nt(rows, cols) * scale
-            grad_cov[...] = part if e == 0 else grad_cov[...] + part
-            rows = jnp.concatenate([xk[n, G:R] for n in blocks], axis=1)
-            cols = jnp.concatenate(
-                [jnp.concatenate([xd[0, n, G:R], xd[1, n, G:R]], axis=0) for n in blocks], axis=1
-            )
-            part = nt(rows, cols) * scale
-            act_cov[...] = part if e == 0 else act_cov[...] + part
+            covariance(grad_cov, 0, G, range(e, e + 4))
+
+    def acts_covariance():
+        for f in range(2):
+            arrived(xd.at[1 - c, f, pl.ds(0, 8), pl.ds(G, A)], ca_r.at[f])
+        for e in (0, 8):
+            covariance(act_cov, G, R, range(e, e + 8))
 
     def correct(distances):
         places = [mod(z + n, 8) for n in distances]
@@ -382,7 +452,7 @@
         copy = pltpu.make_async_copy(grad_cov, grad_out, own_sem.at[3])
         copy.start() if act else copy.wait()
 
-    work = {}
+    work = {ACTS_AT - 7: [functools.partial(acts_over_x, True)], ACTS_AT - 5: [acts_to_planes]}
     for n, when in enumerate(GATHER_AT):
         work.setdefault(when, []).append(functools.partial(columns_hop, n + 1))
     for n in range(4):
@@ -394,12 +464,16 @@
 
     def step(i, carry):
         for f in range(2):
-            for late, fn in ((0, spread), (K1, across), (K2, share)):
+            for late, fn in ((K2, share), (K1, across), (0, spread)):
                 valid, e = stage(f, i, late)
 
                 @pl.when(valid)
                 def _():
                     fn(f, e, True)
+
+            @pl.when(i == ACTS_AT + 2 * hops[f])
+            def _():
+                acts_spread(f, True)
 
         g = i - PROJECT
 
@@ -438,20 +512,29 @@
     in_gather_x(True)
     covariances(8)
     store(True)
+    acts_across(True)
     squares_hop(2)
     in_share(True)
     squares_hop(3)
+    acts_share(True)
     arrived(si.at[1 - c], in_r.at[17])
     correct((0, 1, 7, 2, 6))
+    acts_covariance()
     squares_hop(4)
     correct((3, 5, 4))
 
     store(False)
     over_x(False)
+    acts_over_x(False)
     for j in range(4):
         to_plane(j, False)
+        to_plane(j, False, 1)
     columns_pair(False)
     upper(False)
+    for f in range(2):
+        acts_spread(f, False)
+    acts_across(False)
+    acts_share(False)
     for h in range(4):
         for j in range(2 if h == 0 else 4):
             reduce_send(False, h, j)
@@ -514,7 +597,8 @@
         scratch_shapes=[
             pltpu.VMEM((NB, R, B), BF16),
             pltpu.VMEM((4, Q, B), BF16),
-            pltpu.VMEM((2, NB, R, B), BF16),
+            pltpu.VMEM((4, U, B), BF16),
+            pltpu.VMEM((2, 2, 8, R, B), BF16),
             pltpu.VMEM((G, 2 * G), BF16),
             pltpu.VMEM((2 * A, A), BF16),
             pltpu.VMEM((G, 2 * G), F32),
@@ -530,7 +614,8 @@
             pltpu.VMEM((4, 4, A, B), F32),
             pltpu.VMEM((4, A, B), F32),
             pltpu.VMEM((2, NB, A, B), BF16),
-            dma((3,)), dma((4,)), dma((4,)), dma((4,)), dma((NB,)), dma((NB,)),
+            dma((3,)), dma((4,)), dma((3,)), dma((4,)), dma((5,)), dma((4,)), dma((4,)), dma((NB,)), dma((NB,)),
+            dma((2,)), dma((2,)), dma((2, 2)), dma((2, 2)), dma((2,)), dma((2,)), dma((2,)), dma((2,)), dma((NB,)),
             dma((2, NB)), dma((2, NB)), dma((NB,)), dma((NB,)), dma((NB,)), dma((NB,)),
             dma, dma, dma((2, 4, 2)), dma((2, 4, 2)), dma((8,)), dma((8,)),
             dma((2, 4, 4)), dma((2, 4, 4)), dma, dma, dma((2, 4, 3)), dma((2, 4, 3)), dma((8,)), dma((8,)),

time: 111 us -> 110 us (level)
  no operation moved by 1% of the time
where the time goes in v4:
time: 110 us
  Pallas kernels  110 us (100%)
    pallas_call x1, Pallas kernels, body(): pl.pallas_call(kernel, out_shape=shapes, in_specs=[vmem, hbm, vmem, hbm],...  107 us
    pallas_call x1, Pallas kernels, body(): pl.pallas_call(settle, out_shape=shapes, in_specs=[hbm] * 3, out_specs=(h...  2.47 us

profile of v4, /device:TPU:1, one launch (start us, length us, event | category | flops | bytes accessed | tf_op | source)
XLA Modules:
  0.0 110.2 jit_solution(16707571396348890878)
XLA Ops:
  0.6 107.1 %ekfac.1 = (f32[128,256]{1,0:T(8,128)}, f32[448,896]{1,0:T(8,128)}, f32[448,256]{1,0:T(8,128)}) custom-call(bf16[128,128]{1,0:T(8,128)(2,1)} %acts.1, bf16[448,128]{1,0:T(8,128)(2,1)} %bitcast.3, bf16[128,256]{1,0:T(8,128)(2,1)} %basis_in.1, bf16[448,896]{1,0:T(8,128)(2,1)} %bitcast.2), custom_call_target="tpu_custom_call" | custom-call | tf_op jit(solution)/shard_map/ekfac/pallas_call | solution.py:592
  107.8 2.5 %settle.1 = (f32[128,256]{1,0:T(8,128)}, f32[448,896]{1,0:T(8,128)}, f32[448,256]{1,0:T(8,128)}) custom-call(f32[128,256]{1,0:T(8,128)} %get-tuple-element.6.refs_0_, f32[448,896]{1,0:T(8,128)} %get-tuple-element.7.refs_1_, f32[448,256]{1,0:T(8,128)} %get-tuple-element.8.refs_2_), custom_call_target="tpu_custom_call" | custom-call | tf_op jit(solution)/shard_map/settle/pallas_call | solution.py:629

commit v5 on v4

--- a/solution.py
+++ b/solution.py
@@ -20,6 +20,7 @@
 NB = 16
 GH = G // 2
 GQ = G // 4
+GS = 336
 
 CHAIN = 2
 K1, K2, K3 = 2, 4, 5
@@ -28,7 +29,7 @@
 GATHER_AT = (3, 6, 9, 12)
 REDUCE_AT = PROJECT + 1
 ACTS_AT = 12
-INPUT_AT = (13, 15)
+INPUT_AT = (12, 15)
 
 
 def mod(a, n):
@@ -166,10 +167,12 @@
 
     def squares_rows(n, h, p):
         if h < 3:
-            return pl.ds(GH, GH) if p == 0 else pl.ds(0, GH)
-        if p == 2:
-            return pl.ds(n * GQ, GQ)
-        return (None if n == 0 else pl.ds(GH, GH)) if p == 0 else (pl.ds(0, GH) if n == 0 else None)
+            low, high = (GS, G) if p == 0 else (0, GS)
+        elif p == 2:
+            low, high = ((0, GS // 32 * 16), (GS // 32 * 16, GS))[n]
+        else:
+            low, high = (((G, G), (GS, G)), ((0, GH), (GH, GS)))[p][n]
+        return None if low == high else pl.ds(low, high - low)
 
     def ring_ref(buf, rows, n, h, p, y, shift):
         zz = mod(z - shift - h, 8) if n == 0 else mod(z + shift + h, 8)
@@ -398,11 +401,11 @@
         ring_send(act, sq, squares_rows, g_s, g_r, h, p, yl if p < 2 else 1 - yl)
 
     def lower(act, zz):
-        ref = sq.at[2 * zz + yl, GH:G]
+        ref = sq.at[2 * zz + yl, GS:G]
         send(act, ref, ref, gb_s.at[zz], gb_r.at[zz], at(yl=1 - yl))
 
     def upper(act):
-        ref = sq.at[dp, 0:GH]
+        ref = sq.at[dp, 0:GS]
         send(act, ref, ref, gp_s, gp_r, at(yl=1 - yl))
 
     def squares_hop(h):
@@ -441,7 +444,7 @@
     def correct(distances):
         places = [mod(z + n, 8) for n in distances]
         for zz in places:
-            arrived(sq.at[2 * zz + 1 - yl, GH:G], gb_r.at[zz])
+            arrived(sq.at[2 * zz + 1 - yl, GS:G], gb_r.at[zz])
         blocks = [2 * zz + y for zz in places for y in range(2)]
         rows = jnp.concatenate([sq[e] for e in blocks], axis=1)
         cols = jnp.concatenate([jnp.concatenate([si[0, e], si[1, e]], axis=0) for e in blocks], axis=1)
@@ -505,7 +508,7 @@
     squares_send(True, 0, 0)
     squares_send(True, 0, 1)
     lower(True, z)
-    arrived(sq.at[partner, 0:GH], gp_r)
+    arrived(sq.at[partner, 0:GS], gp_r)
     squares_send(True, 0, 2)
     in_square(True)
     squares_hop(1)

time: 110 us -> 112 us (1.018)
    pallas_call x1, Pallas kernels: 107 us -> 109 us  [body(): pl.pallas_call(kernel, out_shape=shapes, in_specs=[vmem, hbm, vmem, hbm],...]
where the time goes in v5:
time: 112 us
  Pallas kernels  111 us (99%)
    pallas_call x1, Pallas kernels, body(): pl.pallas_call(kernel, out_shape=shapes, in_specs=[vmem, hbm, vmem, hbm],...  109 us
    pallas_call x1, Pallas kernels, body(): pl.pallas_call(settle, out_shape=shapes, in_specs=[hbm] * 3, out_specs=(h...  2.47 us

profile of v5, /device:TPU:1, one launch (start us, length us, event | category | flops | bytes accessed | tf_op | source)
XLA Modules:
  0.0 112.0 jit_solution(2513236174847476069)
XLA Ops:
  0.6 108.9 %ekfac.1 = (f32[128,256]{1,0:T(8,128)}, f32[448,896]{1,0:T(8,128)}, f32[448,256]{1,0:T(8,128)}) custom-call(bf16[128,128]{1,0:T(8,128)(2,1)} %acts.1, bf16[448,128]{1,0:T(8,128)(2,1)} %bitcast.3, bf16[128,256]{1,0:T(8,128)(2,1)} %basis_in.1, bf16[448,896]{1,0:T(8,128)(2,1)} %bitcast.2), custom_call_target="tpu_custom_call" | custom-call | tf_op jit(solution)/shard_map/ekfac/pallas_call | solution.py:595
  109.5 2.5 %settle.1 = (f32[128,256]{1,0:T(8,128)}, f32[448,896]{1,0:T(8,128)}, f32[448,256]{1,0:T(8,128)}) custom-call(f32[128,256]{1,0:T(8,128)} %get-tuple-element.6.refs_0_, f32[448,896]{1,0:T(8,128)} %get-tuple-element.7.refs_1_, f32[448,256]{1,0:T(8,128)} %get-tuple-element.8.refs_2_), custom_call_target="tpu_custom_call" | custom-call | tf_op jit(solution)/shard_map/settle/pallas_call | solution.py:632
